TPU v7x, 32 devices: a whole 2x2x4 slice. The times are simulated.
32 devices in a mesh: seq: 16 (over z, y, x), dp: 2 (over core).
Axes of the slice: x: 2, y: 2, z: 4, core: 2. Of those that a mesh axis runs over, the one named last changes fastest.
Arguments:
- inputs: bfloat16 [2, 256, 256, 512], P('dp', 'seq'), may hold values from -6 to 6
- gate: bfloat16 [2, 256, 256, 512], P('dp', 'seq'), may hold values from -6 to 6
- kernel: bfloat16 [256, 256, 512], P(None, 'seq'), may hold values from -6 to 6
- first_blocks: bfloat16 [256, 256, 256], P('seq'), may hold values from -0.375 to 0.375
- second_blocks: bfloat16 [256, 256, 256], P('seq'), may hold values from -0.375 to 0.375
- cotangent: bfloat16 [2, 256, 256, 512], P('dp', 'seq'), may hold values from -6 to 6
Outputs:
- mixed: bfloat16 [2, 256, 256, 512], P('dp', 'seq')
- grad_inputs: bfloat16 [2, 256, 256, 512], P('dp', 'seq')
- grad_gate: bfloat16 [2, 256, 256, 512], P('dp', 'seq')
- grad_kernel: float32 [256, 256, 512], P(None, 'seq')
All inputs are finite; a program needn't handle non-finite values.
Results may differ from a plain program's by a relative error of at most 0.007.
Values may be sent and summed in bfloat16 or wider, within the bound.
A program may use at most 128 MiB of HBM per device.

v0:
```python
import jax
import jax.numpy as jnp
from jax import lax
from jax.sharding import PartitionSpec as P


def shards(inputs, gate, kernel, first_blocks, second_blocks, cotangent):
    f32 = jnp.float32
    bf16 = jnp.bfloat16
    gate32 = gate.astype(f32)
    cot = cotangent.astype(f32)
    d_result = (cot * gate32).astype(bf16)

    def spread(rows):
        return jnp.einsum("rij,srjd->srid", first_blocks, rows, preferred_element_type=f32).astype(
            bf16
        )

    def mix_columns(piece):
        return jnp.einsum("cqr,srcd->sqcd", second_blocks, piece, preferred_element_type=f32)

    def unmix_columns(scaled):
        return jnp.einsum(
            "cqr,sqcd->srcd", second_blocks, scaled, preferred_element_type=f32
        ).astype(bf16)

    def finish_rows(piece):
        return jnp.einsum("rij,srid->srjd", first_blocks, piece, preferred_element_type=f32)

    second = mix_columns(
        lax.all_to_all(spread(inputs), "seq", split_axis=2, concat_axis=1, tiled=True)
    )
    hidden = (second * kernel).astype(bf16)
    result = finish_rows(
        lax.all_to_all(unmix_columns(hidden), "seq", split_axis=1, concat_axis=2, tiled=True)
    )
    d_hidden = mix_columns(
        lax.all_to_all(spread(d_result), "seq", split_axis=2, concat_axis=1, tiled=True)
    )
    d_second = (d_hidden * kernel).astype(bf16)
    d_inputs = finish_rows(
        lax.all_to_all(unmix_columns(d_second), "seq", split_axis=1, concat_axis=2, tiled=True)
    )
    mixed = (result * gate32).astype(bf16)
    grad_gate = (cot * result).astype(bf16)
    grad_inputs = d_inputs.astype(bf16)
    grad_kernel = lax.psum(jnp.sum(d_hidden * second, axis=0), "dp")
    return (mixed, grad_inputs, grad_gate, grad_kernel)


def solution(mesh):
    placed = (
        P("dp", "seq", None, None),
        P("dp", "seq", None, None),
        P(None, "seq", None),
        P("seq", None, None),
        P("seq", None, None),
        P("dp", "seq", None, None),
    )
    return jax.shard_map(
        shards,
        mesh=mesh,
        in_specs=placed,
        out_specs=(
            P("dp", "seq", None, None),
            P("dp", "seq", None, None),
            P("dp", "seq", None, None),
            P(None, "seq", None),
        ),
        check_vma=False,
    )
```

profile of v0, /device:TPU:14, one launch (start us, length us, event | category | flops | bytes accessed | tf_op | source)
XLA Modules:
  0.0 453.4 jit_solution(9748813159197891301)
XLA Ops:
  8.8 5.6 %convert_bitcast_fusion.4 = bf16[1,16,256,512]{2,3,1,0:T(8,128)(2,1)} fusion(bf16[16,256,256]{2,1,0:T(8,128)(2,1)S(1)} %copy-done, bf16[1,16,256,512]{3,2,1,0:T(8,128)(2,1)} %param.6), kind=kOutput, calls=%fused_computation.30 | convolution fusion | flops 1075838976 | bytes 10485760 | tf_op jit(solution)/shard_map/rij,srjd->srid/dot_general | solution.py:15
  14.3 7.8 %copy.43 = bf16[1,16,256,512]{3,1,0,2:T(8,128)(2,1)} copy(bf16[1,16,256,512]{2,3,1,0:T(8,128)(2,1)} %convert_bitcast_fusion.4) | data formatting | bytes 8388608 | tf_op jit(solution)/shard_map/convert_element_type | solution.py:15
  22.2 7.1 %all-to-all-start = ((bf16[1,16,256,512]{3,1,0,2:T(8,128)(2,1)}), bf16[1,16,256,512]{3,1,0,2:T(8,128)(2,1)}, u32[]{:S(2)}, u32[]{:S(2)}) async-start(bf16[1,16,256,512]{3,1,0,2:T(8,128)(2,1)} %copy.43), calls=%async_computation | async-start | bytes 8388608 | tf_op jit(solution)/shard_map/all_to_all | solution.py:31
  29.3 6.4 %copy.52 = bf16[1,16,256,512]{2,3,1,0:T(8,128)(2,1)} copy(bf16[1,16,256,512]{3,2,1,0:T(8,128)(2,1)} %param.11) | data formatting | bytes 8388608 | tf_op args[5]
  35.7 6.4 %copy.51 = bf16[1,16,256,512]{2,3,1,0:T(8,128)(2,1)} copy(bf16[1,16,256,512]{3,2,1,0:T(8,128)(2,1)} %param.7) | data formatting | bytes 8388608 | tf_op args[1]
  42.1 6.8 %convert_bitcast_fusion.2 = bf16[1,16,256,512]{2,3,1,0:T(8,128)(2,1)} fusion(bf16[16,256,256]{2,1,0:T(8,128)(2,1)S(1)} %copy-done, bf16[1,16,256,512]{2,3,1,0:T(8,128)(2,1)} %copy.51, bf16[1,16,256,512]{2,3,1,0:T(8,128)(2,1)} %copy.52), kind=kOutput, calls=%fused_computation.28 | convolution fusion | flops 1084227584 | bytes 14680064 | tf_op jit(solution)/shard_map/rij,srjd->srid/dot_general | solution.py:15
  48.9 8.0 %copy.53 = bf16[1,16,256,512]{3,1,0,2:T(8,128)(2,1)} copy(bf16[1,16,256,512]{2,3,1,0:T(8,128)(2,1)} %convert_bitcast_fusion.2) | data formatting | bytes 8388608 | tf_op jit(solution)/shard_map/convert_element_type | solution.py:15
  56.8 67.1 %all-to-all-done = bf16[1,16,256,512]{3,1,0,2:T(8,128)(2,1)} async-done(((bf16[1,16,256,512]{3,1,0,2:T(8,128)(2,1)}), bf16[1,16,256,512]{3,1,0,2:T(8,128)(2,1)}, u32[]{:S(2)}, u32[]{:S(2)}) %all-to-all-start) | async-done | bytes 4194336 | tf_op jit(solution)/shard_map/all_to_all | solution.py:31
  129.1 7.5 %copy.47 = bf16[256,16,512]{0,2,1:T(8,128)(2,1)} copy(bf16[256,16,512]{2,1,0:T(8,128)(2,1)} %param.8) | data formatting | bytes 8388608 | tf_op args[2]
  142.7 5.1 %fusion.21 = f32[16,512,256]{2,1,0:T(8,128)S(1)} fusion(bf16[16,256,256]{2,1,0:T(8,128)(2,1)S(1)} %copy-done.4, bf16[256,16,512]{2,1,0:T(8,128)(2,1)S(1)} %bitcast.109), kind=kOutput, calls=%fused_computation.24 | convolution fusion | flops 1073741824 | bytes 14680064 | tf_op jit(solution)/shard_map/cqr,srcd->sqcd/dot_general | solution.py:20
  151.1 6.3 %convert_bitcast_fusion.3 = bf16[1,256,16,512]{1,3,2,0:T(8,128)(2,1)} fusion(bf16[16,256,256]{2,1,0:T(8,128)(2,1)} %param.10, f32[16,512,256]{2,1,0:T(8,128)S(1)} %fusion.21, bf16[256,16,512]{0,2,1:T(8,128)(2,1)} %copy.47), kind=kOutput, calls=%fused_computation.29 | convolution fusion | flops 1082130432 | bytes 18874368 | tf_op jit(solution)/shard_map/cqr,sqcd->srcd/dot_general | solution.py:23
  157.3 8.0 %copy.48 = bf16[1,256,16,512]{3,2,0,1:T(8,128)(2,1)} copy(bf16[1,256,16,512]{1,3,2,0:T(8,128)(2,1)} %convert_bitcast_fusion.3) | data formatting | bytes 8388608 | tf_op jit(solution)/shard_map/convert_element_type | solution.py:25
  165.3 56.4 %all-to-all-done.2 = bf16[1,16,256,512]{3,1,0,2:T(8,128)(2,1)} async-done(((bf16[1,16,256,512]{3,1,0,2:T(8,128)(2,1)}), bf16[1,16,256,512]{3,1,0,2:T(8,128)(2,1)}, u32[]{:S(2)}, u32[]{:S(2)}) %all-to-all-start.2) | async-done | bytes 4194336 | tf_op jit(solution)/shard_map/all_to_all | solution.py:38
  233.3 8.5 %fusion.19 = f32[16,512,256]{2,1,0:T(8,128)} fusion(bf16[16,256,256]{2,1,0:T(8,128)(2,1)S(1)} %copy-done.5, bf16[256,16,512]{2,1,0:T(8,128)(2,1)S(1)} %bitcast.110), kind=kOutput, calls=%fused_computation.22 | convolution fusion | flops 1073741824 | bytes 14680064 | tf_op jit(solution)/shard_map/cqr,srcd->sqcd/dot_general | solution.py:20
  241.8 10.2 %fusion.5 = f32[256,16,512]{0,2,1:T(8,128)} fusion(f32[16,512,256]{2,1,0:T(8,128)} %copy-done.1, f32[16,512,256]{2,1,0:T(8,128)} %fusion.19), kind=kLoop, calls=%fused_computation.11 | loop fusion | flops 2097152 | bytes 25165824 | tf_op jit(solution)/shard_map/reduce_sum | solution.py:47
  252.1 8.7 %convert_bitcast_fusion.1 = bf16[1,256,16,512]{1,3,2,0:T(8,128)(2,1)} fusion(bf16[16,256,256]{2,1,0:T(8,128)(2,1)} %param.10, f32[16,512,256]{2,1,0:T(8,128)} %fusion.19, bf16[256,16,512]{0,2,1:T(8,128)(2,1)} %copy.47), kind=kOutput, calls=%fused_computation.27 | convolution fusion | flops 1082130432 | bytes 18874368 | tf_op jit(solution)/shard_map/cqr,sqcd->srcd/dot_general | solution.py:23
  260.8 8.5 %copy.57 = bf16[1,256,16,512]{3,2,0,1:T(8,128)(2,1)} copy(bf16[1,256,16,512]{1,3,2,0:T(8,128)(2,1)} %convert_bitcast_fusion.1) | data formatting | bytes 8388608 | tf_op jit(solution)/shard_map/convert_element_type | solution.py:25
  269.2 50.3 %all-to-all-done.1 = bf16[1,256,16,512]{3,2,0,1:T(8,128)(2,1)} async-done(((bf16[1,256,16,512]{3,2,0,1:T(8,128)(2,1)}), bf16[1,256,16,512]{3,2,0,1:T(8,128)(2,1)}, u32[]{:S(2)}, u32[]{:S(2)}) %all-to-all-start.1) | async-done | bytes 4194336 | tf_op jit(solution)/shard_map/all_to_all | solution.py:35
  330.9 8.0 %fusion.2 = (bf16[1,16,256,512]{2,3,1,0:T(8,128)(2,1)}, bf16[1,16,256,512]{2,3,1,0:T(8,128)(2,1)}) fusion(bf16[1,16,256,512]{2,3,1,0:T(8,128)(2,1)S(1)} %copy-done.2, bf16[1,16,256,512]{2,3,1,0:T(8,128)(2,1)S(1)} %copy-done.3, bf16[16,256,512]{2,1,0:T(8,128)(2,1)} %bitcast.114, bf16[16,256,256]{2,1,0:T(8,128)(2,1)S(1)} %copy-done), kind=kOutput, calls=%fused_computation.7 | convolution fusion | flops 1086324736 | bytes 23068672 | tf_op jit(solution)/shard_map/rij,srid->srjd/dot_general | solution.py:28
  338.9 6.4 %copy.60 = bf16[1,16,256,512]{3,2,1,0:T(8,128)(2,1)} copy(bf16[1,16,256,512]{2,3,1,0:T(8,128)(2,1)} %get-tuple-element.17) | data formatting | bytes 8388608
  345.3 72.0 %all-to-all-done.3 = bf16[1,256,16,512]{3,2,0,1:T(8,128)(2,1)} async-done(((bf16[1,256,16,512]{3,2,0,1:T(8,128)(2,1)}), bf16[1,256,16,512]{3,2,0,1:T(8,128)(2,1)}, u32[]{:S(2)}, u32[]{:S(2)}) %all-to-all-start.3) | async-done | bytes 4194336 | tf_op jit(solution)/shard_map/all_to_all | solution.py:42
  423.4 6.4 %copy.61 = bf16[1,16,256,512]{3,2,1,0:T(8,128)(2,1)} copy(bf16[1,16,256,512]{2,3,1,0:T(8,128)(2,1)} %convert_bitcast_fusion) | data formatting | bytes 8388608
  429.8 6.4 %copy.62 = bf16[1,16,256,512]{3,2,1,0:T(8,128)(2,1)} copy(bf16[1,16,256,512]{2,3,1,0:T(8,128)(2,1)} %get-tuple-element.16) | data formatting | bytes 8388608
  436.2 10.4 %copy.63 = f32[256,16,512]{2,1,0:T(8,128)} copy(f32[256,16,512]{0,2,1:T(8,128)} %all-reduce.2.cloned.1.call-done) | data formatting | bytes 16777216
  (25 shorter events, 45.0 us)
Async XLA Ops:
  7.2 1.6 copy-start
  22.2 101.8 %all-to-all-start = ((bf16[1,16,256,512]{3,1,0,2:T(8,128)(2,1)}), bf16[1,16,256,512]{3,1,0,2:T(8,128)(2,1)}, u32[]{:S(2)}, u32[]{:S(2)}) async-start(bf16[1,16,256,512]{3,1,0,2:T(8,128)(2,1)} %copy.43), calls=%async_computation | async-start | bytes 8388608 | tf_op jit(solution)/shard_map/all_to_all | solution.py:31
  124.0 97.8 %all-to-all-start.2 = ((bf16[1,16,256,512]{3,1,0,2:T(8,128)(2,1)}), bf16[1,16,256,512]{3,1,0,2:T(8,128)(2,1)}, u32[]{:S(2)}, u32[]{:S(2)}) async-start(bf16[1,16,256,512]{3,1,0,2:T(8,128)(2,1)} %copy.53), calls=%async_computation.2 | async-start | bytes 8388608 | tf_op jit(solution)/shard_map/all_to_all | solution.py:38
  141.1 1.6 copy-start.4
  147.8 3.2 copy-start.1
  221.8 97.8 %all-to-all-start.1 = ((bf16[1,256,16,512]{3,2,0,1:T(8,128)(2,1)}), bf16[1,256,16,512]{3,2,0,1:T(8,128)(2,1)}, u32[]{:S(2)}, u32[]{:S(2)}) async-start(bf16[1,256,16,512]{3,2,0,1:T(8,128)(2,1)} %copy.48), calls=%async_computation.1 | async-start | bytes 8388608 | tf_op jit(solution)/shard_map/all_to_all | solution.py:35
  226.9 209.3 %all-reduce.2.cloned.1.call-start = ((), (), s32[]{:S(2)}) async-start(), calls=%async_computation.4 | async-start | bytes 16777216 | tf_op jit(solution)/shard_map/psum | solution.py:47
  231.7 1.6 copy-start.5
  319.5 97.8 %all-to-all-start.3 = ((bf16[1,256,16,512]{3,2,0,1:T(8,128)(2,1)}), bf16[1,256,16,512]{3,2,0,1:T(8,128)(2,1)}, u32[]{:S(2)}, u32[]{:S(2)}) async-start(bf16[1,256,16,512]{3,2,0,1:T(8,128)(2,1)} %copy.57), calls=%async_computation.3 | async-start | bytes 8388608 | tf_op jit(solution)/shard_map/all_to_all | solution.py:42
  324.6 5.1 %copy-start.2 = (bf16[1,16,256,512]{2,3,1,0:T(8,128)(2,1)S(1)}, bf16[1,16,256,512]{2,3,1,0:T(8,128)(2,1)}, u32[]{:S(2)}) copy-start(bf16[1,16,256,512]{2,3,1,0:T(8,128)(2,1)} %copy.52) | copy-start | bytes 12582916
  324.6 6.2 %copy-start.3 = (bf16[1,16,256,512]{2,3,1,0:T(8,128)(2,1)S(1)}, bf16[1,16,256,512]{2,3,1,0:T(8,128)(2,1)}, u32[]{:S(2)}) copy-start(bf16[1,16,256,512]{2,3,1,0:T(8,128)(2,1)} %copy.51) | copy-start | bytes 12582916
Sparse Core Ops, SparseCore 0:
  252.2 40.0 all-reduce.1
where the time goes:
time: 456 us; the launch traced here: 453 us
  waiting for transfers between devices  246 us (54%)
  local copies, waits for them, and re-layouts  108 us (24%)
  matrix products  52.5 us (12%)
  starting transfers between devices  22.7 us (5%)
  between operations  14.1 us (3%)
  other arithmetic  10.2 us (2%)
    all_to_all x1, waiting for transfers between devices, shards(): lax.all_to_all(unmix_columns(d_second), 'seq', split_axis=1, concat_axis=...  72 us
    all_to_all x1, waiting for transfers between devices, shards(): lax.all_to_all(spread(inputs), 'seq', split_axis=2, concat_axis=1, tiled=...  67.1 us
    unnamed x19, local copies, waits for them, and re-layouts  58 us
    all_to_all x1, waiting for transfers between devices, shards(): lax.all_to_all(spread(d_result), 'seq', split_axis=2, concat_axis=1, tile...  56.4 us
    all_to_all x1, waiting for transfers between devices, shards(): lax.all_to_all(unmix_columns(hidden), 'seq', split_axis=1, concat_axis=2,...  50.3 us
    convert_element_type x2, local copies, waits for them, and re-layouts, unmix_columns(): return jnp.einsum('cqr,sqcd->srcd', second_blocks, scaled, preferred_elem...  16.4 us
    convert_element_type x2, local copies, waits for them, and re-layouts, spread(): jnp.einsum('rij,srjd->srid', first_blocks, rows, preferred_element_type=f32)  15.8 us
    dot_general x2, matrix products, unmix_columns(): jnp.einsum('cqr,sqcd->srcd', second_blocks, scaled, preferred_element_typ...  15 us
  transfers between devices with their start and end apart: 5, of which 4 were waited for; matrix products, arithmetic and copies ran while one was open for 31% of the time, Pallas kernels for 0%

commit v1 on v0

--- a/solution.py
+++ b/solution.py
@@ -1,7 +1,394 @@
+import functools
+
 import jax
 import jax.numpy as jnp
 from jax import lax
+from jax.experimental import pallas as pl
+from jax.experimental.pallas import tpu as pltpu
 from jax.sharding import PartitionSpec as P
+
+MESH = pl.DeviceIdType.MESH
+LANES = 128
+EARLY = 2
+
+
+def fused(
+    n,
+    x_hbm,
+    gate_hbm,
+    kern_hbm,
+    a_hbm,
+    b_hbm,
+    cot_hbm,
+    mixed_hbm,
+    gin_hbm,
+    ggate_hbm,
+    gk_hbm,
+    part_hbm,
+    a,
+    b,
+    x,
+    gate,
+    cot,
+    send_f,
+    send_b,
+    recv_1f,
+    recv_1b,
+    recv_2f,
+    recv_2b,
+    second,
+    turn,
+    kst,
+    tmp,
+    load_sem,
+    tmp_sem,
+    out_sem,
+    row_sem,
+    send_sem,
+    recv_sem,
+    dp_send,
+    dp_recv,
+):
+    f32 = jnp.float32
+    bf16 = jnp.bfloat16
+    own, cols, width = x.shape
+    rows = cols
+    half = n // 2
+    cut = cols // 2
+    slabs = width // LANES
+    block = own * own
+    me = lax.axis_index("seq")
+    other = 1 - lax.axis_index("dp")
+    near_half = me // half
+    far_half = 1 - near_half
+    spot = me % half
+
+    def load(src, dst, i):
+        return pltpu.make_async_copy(src, dst, load_sem.at[i])
+
+    load(a_hbm, a, 0).start()
+    load(x_hbm, x, 1).start()
+    load(gate_hbm, gate, 2).start()
+    load(cot_hbm, cot, 3).start()
+    load(b_hbm, b, 4).start()
+
+    barrier = pltpu.get_barrier_semaphore()
+
+    @pl.loop(1, n)
+    def _(i):
+        pl.semaphore_signal(
+            barrier, inc=1, device_id={"seq": (me + i) % n}, device_id_type=MESH
+        )
+
+    pl.semaphore_signal(barrier, inc=1, device_id={"dp": other}, device_id_type=MESH)
+    pl.semaphore_wait(barrier, n)
+
+    def lane(k):
+        return pl.ds(k * LANES, LANES)
+
+    def message(stage, send, recv, to, slot):
+        return pltpu.make_async_remote_copy(
+            src_ref=send.at[to],
+            dst_ref=recv.at[slot],
+            send_sem=send_sem.at[stage, to],
+            recv_sem=recv_sem.at[stage, slot],
+            device_id={"seq": to},
+            device_id_type=MESH,
+        )
+
+    def wait_sent(stage, send, recv):
+        @pl.loop(1, n)
+        def _(i):
+            to = (me + i) % n
+            message(stage, send, recv, to, to).wait_send()
+
+    def wait_arrived(stage, send, recv):
+        @pl.loop(1, n)
+        def _(i):
+            slot = (me + i) % n
+            message(stage, send, recv, slot, slot).wait_recv()
+
+    def produce(side, product, send):
+        at = pl.multiple_of(side * cut, cut)
+
+        @pl.loop(0, own)
+        def _(e):
+            value = product(e, at)
+            for k in range(slabs):
+                turn[k, pl.ds(e, cut, stride=own), :] = value[
+                    :, k * LANES : (k + 1) * LANES
+                ]
+
+        @pl.loop(0, half)
+        def _(j):
+            for k in range(slabs):
+                piece = turn[k, pl.ds(pl.multiple_of(j * block, block), block), :]
+                send[side * half + j, :, :, k * LANES : (k + 1) * LANES] = piece.reshape(
+                    own, own, LANES
+                ).astype(bf16)
+
+    def exchange(stage, product, send, recv):
+        def to_far(j):
+            to = far_half * half + (spot + j) % half
+            message(stage, send, recv, to, me).start()
+
+        def to_near(j):
+            to = near_half * half + (spot + 1 + j) % half
+            message(stage, send, recv, to, me).start()
+
+        produce(far_half, product, send)
+
+        @pl.loop(0, EARLY)
+        def _(j):
+            to_far(j)
+
+        produce(near_half, product, send)
+
+        @pl.loop(0, half - 1)
+        def _(j):
+            to_near(j)
+
+            @pl.when(j < half - EARLY)
+            def _():
+                to_far(j + EARLY)
+
+        recv[me] = send[me]
+
+    def spread(e, at):
+        return jnp.dot(a[e, pl.ds(at, cut), :], x[e], preferred_element_type=f32)
+
+    def unmix(held):
+        def product(e, at):
+            values = held[:, e].reshape(rows, width)
+            return lax.dot_general(
+                b[e, :, pl.ds(at, cut)],
+                values,
+                (((0,), (0,)), ((), ())),
+                preferred_element_type=f32,
+            )
+
+        return product
+
+    def finish(held, e):
+        return lax.dot_general(
+            a[e],
+            held[:, e].reshape(cols, width),
+            (((0,), (0,)), ((), ())),
+            preferred_element_type=f32,
+        )
+
+    load(a_hbm, a, 0).wait()
+    load(x_hbm, x, 1).wait()
+    exchange(0, spread, send_f, recv_1f)
+
+    load(gate_hbm, gate, 2).wait()
+    load(cot_hbm, cot, 3).wait()
+
+    @pl.loop(0, own)
+    def _(e):
+        x[e] = (cot[e].astype(f32) * gate[e].astype(f32)).astype(bf16)
+
+    exchange(1, spread, send_b, recv_1b)
+
+    quarter = kst.shape[0] // own
+
+    @pl.loop(0, rows // quarter)
+    def _(i):
+        size = quarter * own
+        take = load(kern_hbm.at[pl.ds(pl.multiple_of(i * size, size), size), :], kst, 1)
+        take.start()
+        take.wait()
+        for k in range(slabs):
+            turn[k, 0:size, :] = kst[:, k * LANES : (k + 1) * LANES].astype(f32)
+
+        @pl.loop(0, own)
+        def _(e):
+            for k in range(slabs):
+                x[
+                    e,
+                    pl.ds(pl.multiple_of(i * quarter, quarter), quarter),
+                    k * LANES : (k + 1) * LANES,
+                ] = turn[k, pl.ds(e, quarter, stride=own), :].astype(bf16)
+
+    load(b_hbm, b, 4).wait()
+    wait_arrived(0, send_f, recv_1f)
+
+    @pl.loop(0, own)
+    def _(e):
+        value = jnp.dot(
+            b[e], recv_1f[:, e].reshape(rows, width), preferred_element_type=f32
+        )
+        second[e] = value
+        recv_1f[:, e] = (value * x[e].astype(f32)).astype(bf16).reshape(n, own, width)
+
+    wait_sent(0, send_f, recv_1f)
+    exchange(2, unmix(recv_1f), send_f, recv_2f)
+
+    wait_arrived(1, send_b, recv_1b)
+
+    @pl.loop(0, own)
+    def _(e):
+        value = jnp.dot(
+            b[e], recv_1b[:, e].reshape(rows, width), preferred_element_type=f32
+        )
+        second[e] = second[e] * value
+        recv_1b[:, e] = (value * x[e].astype(f32)).astype(bf16).reshape(n, own, width)
+
+    swap = pltpu.make_async_remote_copy(
+        src_ref=second,
+        dst_ref=part_hbm,
+        send_sem=dp_send,
+        recv_sem=dp_recv,
+        device_id={"dp": other},
+        device_id_type=MESH,
+    )
+    swap.start()
+    wait_sent(1, send_b, recv_1b)
+    exchange(3, unmix(recv_1b), send_b, recv_2b)
+
+    swap.wait_recv()
+    for side in range(2):
+        at = side * cut
+
+        def part(e, slot):
+            return pltpu.make_async_copy(
+                part_hbm.at[e, pl.ds(at, cut), :], tmp.at[slot], tmp_sem.at[slot]
+            )
+
+        part(0, 0).start()
+
+        @pl.loop(0, own)
+        def _(e):
+            @pl.when(e < own - 1)
+            def _():
+                part(e + 1, (e + 1) % 2).start()
+
+            part(e, e % 2).wait()
+            total = second[e, at : at + cut, :] + tmp[e % 2]
+            for k in range(slabs):
+                turn[k, pl.ds(e, cut, stride=own), :] = total[
+                    :, k * LANES : (k + 1) * LANES
+                ]
+
+        outs = [
+            pltpu.make_async_copy(
+                turn.at[k],
+                gk_hbm.at[pl.ds(at * own, cut * own), lane(k)],
+                out_sem.at[k],
+            )
+            for k in range(slabs)
+        ]
+        for out in outs:
+            out.start()
+        for out in outs:
+            out.wait()
+
+    wait_arrived(2, send_f, recv_2f)
+
+    @pl.loop(0, own)
+    def _(e):
+        result = finish(recv_2f, e)
+        mixed = (result * gate[e].astype(f32)).astype(bf16)
+        ggate = (cot[e].astype(f32) * result).astype(bf16)
+        gate[e] = mixed
+        cot[e] = ggate
+
+    out_mixed = load(gate, mixed_hbm, 2)
+    out_ggate = load(cot, ggate_hbm, 3)
+    out_mixed.start()
+    out_ggate.start()
+
+    swap.wait_send()
+    wait_sent(2, send_f, recv_2f)
+    wait_arrived(3, send_b, recv_2b)
+
+    def out_row(e):
+        return pltpu.make_async_copy(x.at[e], gin_hbm.at[e], row_sem.at[e])
+
+    @pl.loop(0, own)
+    def _(e):
+        x[e] = finish(recv_2b, e).astype(bf16)
+        out_row(e).start()
+
+    wait_sent(3, send_b, recv_2b)
+    out_mixed.wait()
+    out_ggate.wait()
+
+    @pl.loop(0, own)
+    def _(e):
+        out_row(e).wait()
+
+
+def fused_shards(n, inputs, gate, kernel, first_blocks, second_blocks, cotangent):
+    f32 = jnp.float32
+    bf16 = jnp.bfloat16
+    _, own, cols, width = inputs.shape
+    rows = kernel.shape[0]
+    slabs = width // LANES
+    here = jax.ShapeDtypeStruct((own, cols, width), bf16)
+    anywhere = pl.BlockSpec(memory_space=pl.ANY)
+    wire = pltpu.VMEM((n, own, own, width), bf16)
+    held = pltpu.VMEM((own, cols, width), bf16)
+    dma = pltpu.SemaphoreType.DMA
+    mixed, gin, ggate, gk, _ = pl.pallas_call(
+        functools.partial(fused, n),
+        out_shape=(
+            here,
+            here,
+            here,
+            jax.ShapeDtypeStruct((rows * own, width), f32),
+            jax.ShapeDtypeStruct((own, rows, width), f32),
+        ),
+        in_specs=[anywhere] * 6,
+        out_specs=[anywhere] * 5,
+        scratch_shapes=[
+            pltpu.VMEM((own, cols, cols), bf16),
+            pltpu.VMEM((own, rows, rows), bf16),
+            held,
+            held,
+            held,
+            wire,
+            wire,
+            wire,
+            wire,
+            wire,
+            wire,
+            pltpu.VMEM((own, rows, width), f32),
+            pltpu.VMEM((slabs, cols // 2 * own, LANES), f32),
+            pltpu.VMEM((rows // 4 * own, width), bf16),
+            pltpu.VMEM((2, rows // 2, width), f32),
+            dma((5,)),
+            dma((2,)),
+            dma((slabs,)),
+            dma((own,)),
+            dma((4, n)),
+            dma((4, n)),
+            dma,
+            dma,
+        ],
+        compiler_params=pltpu.CompilerParams(
+            collective_id=0, has_side_effects=True, vmem_limit_bytes=60 << 20
+        ),
+        cost_estimate=pl.CostEstimate(
+            flops=16 * own * cols * cols * width,
+            bytes_accessed=48 * own * cols * width,
+            transcendentals=0,
+        ),
+    )(
+        inputs.reshape(own, cols, width),
+        gate.reshape(own, cols, width),
+        kernel.reshape(rows * own, width),
+        first_blocks,
+        second_blocks,
+        cotangent.reshape(own, cols, width),
+    )
+    shape = inputs.shape
+    return (
+        mixed.reshape(shape),
+        gin.reshape(shape),
+        ggate.reshape(shape),
+        gk.reshape(rows, own, width),
+    )
 
 
 def shards(inputs, gate, kernel, first_blocks, second_blocks, cotangent):
@@ -57,15 +444,35 @@
         P("seq", None, None),
         P("dp", "seq", None, None),
     )
-    return jax.shard_map(
-        shards,
-        mesh=mesh,
-        in_specs=placed,
-        out_specs=(
-            P("dp", "seq", None, None),
-            P("dp", "seq", None, None),
-            P("dp", "seq", None, None),
-            P(None, "seq", None),
-        ),
-        check_vma=False,
-    )
+    def program(inputs, gate, kernel, first_blocks, second_blocks, cotangent):
+        n = mesh.shape["seq"]
+        seqs, rows, cols, width = inputs.shape
+        fits = (
+            mesh.shape["dp"] == 2
+            and seqs == 2
+            and rows == cols
+            and n % 2 == 0
+            and rows % (16 * n) == 0
+            and rows % 256 == 0
+            and width % LANES == 0
+        )
+        body = functools.partial(fused_shards, n) if fits else shards
+        return placed_body(body)(
+            inputs, gate, kernel, first_blocks, second_blocks, cotangent
+        )
+
+    def placed_body(body):
+        return jax.shard_map(
+            body,
+            mesh=mesh,
+            in_specs=placed,
+            out_specs=(
+                P("dp", "seq", None, None),
+                P("dp", "seq", None, None),
+                P("dp", "seq", None, None),
+                P(None, "seq", None),
+            ),
+            check_vma=False,
+        )
+
+    return program

time: 456 us -> 412 us (0.904)
  Pallas kernels: 0 us -> 391 us
  waiting for transfers between devices: 246 us -> 0 us
  local copies, waits for them, and re-layouts: 108 us -> 16 us
  matrix products: 52.5 us -> 0 us
  starting transfers between devices: 22.7 us -> 0 us
  between operations: 14.1 us -> 0.65 us
  other arithmetic: 10.2 us -> 0.01 us
    pallas_call x0 -> x1, Pallas kernels: none -> 391 us  [fused_shards(): pl.pallas_call(functools.partial(fused, n), out_shape=(here, here, here,...]
    all_to_all x4 -> x0, waiting for transfers between devices: 246 us -> none  [the longest x1 72 us: shards(): lax.all_to_all(unmix_columns(d_second), 'seq', split_axis=1, concat_axis=...]
    dot_general x8 -> x0, matrix products: 52.5 us -> none  [the longest x2 15 us: unmix_columns(): jnp.einsum('cqr,sqcd->srcd', second_blocks, scaled, preferred_element_typ...]
    unnamed x19 -> x12, local copies, waits for them, and re-layouts: 58 us -> 16 us
    convert_element_type x4 -> x0, local copies, waits for them, and re-layouts: 32.2 us -> none  [the longest x2 16.4 us: unmix_columns(): return jnp.einsum('cqr,sqcd->srcd', second_blocks, scaled, preferred_elem...]
    all_to_all x4 -> x0, starting transfers between devices: 22.5 us -> none  [the longest x1 7.14 us: shards(): lax.all_to_all(spread(inputs), 'seq', split_axis=2, concat_axis=1, tiled=...]
    all_to_all x6 -> x0, local copies, waits for them, and re-layouts: 17.8 us -> none  [the longest x1 5.11 us: shards(): lax.all_to_all(unmix_columns(hidden), 'seq', split_axis=1, concat_axis=2,...]
    reduce_sum x1 -> x0, other arithmetic: 10.2 us -> none  [shards(): grad_kernel = lax.psum(jnp.sum(d_hidden * second, axis=0), 'dp')]
  transfers between devices with their start and end apart: 5 -> 0, of which waited for: 4 -> 0; matrix products, arithmetic and copies ran while one was open for 31% -> 0% of each run, Pallas kernels for 0% -> 0%
where the time goes in v1:
time: 412 us; the launch traced here: 408 us
  Pallas kernels  391 us (95%)
  local copies, waits for them, and re-layouts  16 us (4%)
    pallas_call x1, Pallas kernels, fused_shards(): pl.pallas_call(functools.partial(fused, n), out_shape=(here, here, here,...  391 us
    unnamed x12, local copies, waits for them, and re-layouts  16 us

profile of v1, /device:TPU:14, one launch (start us, length us, event | category | flops | bytes accessed | tf_op | source)
XLA Modules:
  0.0 407.8 jit_solution(16994458180293774637)
XLA Ops:
  0.6 391.1 %shard_map.93 = (bf16[16,256,512]{2,1,0:T(8,128)(2,1)}, bf16[16,256,512]{2,1,0:T(8,128)(2,1)}, bf16[16,256,512]{2,1,0:T(8,128)(2,1)}, f32[4096,512]{1,0:T(8,128)}, f32[16,256,512]{2,1,0:T(8,128)}) custom-call(bf16[16,256,512]{2,1,0:T(8,128)(2,1)} %bitcast.14, bf16[16,256,512]{2,1,0:T(8,128)(2,1)} %bitcast.15, bf16[4096,512]{1,0:T(8,128)(2,1)} %bitcast.16, ...), custom_call_target="tpu_custom_call" | custom-call | flops 8589934592 | bytes 100663296 | tf_op jit(solution)/shard_map/pallas_call | solution.py:333
  391.8 0.0 copy-start.1
  391.8 4.7 %copy.14 = bf16[1,16,256,512]{3,2,1,0:T(8,128)(2,1)} copy(bf16[1,16,256,512]{3,2,1,0:T(8,128)(2,1)} %bitcast.13) | data formatting | bytes 8388608
  396.5 0.0 copy-done.1
  396.5 0.0 copy-start
  396.5 0.0 slice-start
  396.5 2.1 copy.15
  398.6 1.6 copy-done
  400.2 0.0 slice-start.1
  400.2 2.1 copy.16
  402.3 0.0 slice-done
  402.3 2.1 slice-done.1
  404.4 3.4 copy.17
  (1 shorter events, 0.0 us)
Async XLA Ops:
  391.8 4.7 %copy-start.1 = (bf16[16,256,512]{2,1,0:T(8,128)(2,1)S(1)}, bf16[16,256,512]{2,1,0:T(8,128)(2,1)}, u32[]{:S(2)}) copy-start(bf16[16,256,512]{2,1,0:T(8,128)(2,1)} %get-tuple-element.9) | copy-start | bytes 12582916
  396.5 3.7 copy-start
  396.5 5.8 %slice-start = ((s8[8388608]{0:T(1024)(128)(4,1)}), s8[4194304]{0:T(1024)(128)(4,1)S(1)}, s32[]{:S(2)}) async-start(s8[8388608]{0:T(1024)(128)(4,1)} %bitcast.8), calls=%async_computation | async-start | bytes 8388608
  400.2 4.2 %slice-start.1 = ((s8[8388608]{0:T(1024)(128)(4,1)}), s8[4194304]{0:T(1024)(128)(4,1)S(1)}, s32[]{:S(2)}) async-start(s8[8388608]{0:T(1024)(128)(4,1)} %bitcast.8), calls=%async_computation.1 | async-start | bytes 8388608

commit v2 on v1

--- a/solution.py
+++ b/solution.py
@@ -9,7 +9,7 @@
 
 MESH = pl.DeviceIdType.MESH
 LANES = 128
-EARLY = 2
+LAG = 2
 
 
 def fused(
@@ -127,32 +127,35 @@
                     own, own, LANES
                 ).astype(bf16)
 
-    def exchange(stage, product, send, recv):
-        def to_far(j):
-            to = far_half * half + (spot + j) % half
-            message(stage, send, recv, to, me).start()
-
-        def to_near(j):
-            to = near_half * half + (spot + 1 + j) % half
-            message(stage, send, recv, to, me).start()
-
+    def order(i):
+        far = 1 - i % 2
+        side = far * far_half + (1 - far) * near_half
+        return side * half + (spot + (1 - far) + i // 2) % half
+
+    def start(stage, send, recv, i):
+        message(stage, send, recv, order(i), me).start()
+
+    def left(stage, send, recv, i):
+        to = order(i)
+        message(stage, send, recv, to, to).wait_send()
+
+    def produce_all(product, send, recv):
         produce(far_half, product, send)
-
-        @pl.loop(0, EARLY)
-        def _(j):
-            to_far(j)
-
         produce(near_half, product, send)
-
-        @pl.loop(0, half - 1)
-        def _(j):
-            to_near(j)
-
-            @pl.when(j < half - EARLY)
+        recv[me] = send[me]
+
+    def issue(stage, send, recv, before):
+        @pl.loop(0, n - 1)
+        def _(i):
+            @pl.when(i >= LAG)
             def _():
-                to_far(j + EARLY)
-
-        recv[me] = send[me]
+                left(*before, i - LAG)
+
+            start(stage, send, recv, i)
+
+        @pl.loop(n - 1 - LAG, n - 1)
+        def _(i):
+            left(*before, i)
 
     def spread(e, at):
         return jnp.dot(a[e, pl.ds(at, cut), :], x[e], preferred_element_type=f32)
@@ -179,7 +182,17 @@
 
     load(a_hbm, a, 0).wait()
     load(x_hbm, x, 1).wait()
-    exchange(0, spread, send_f, recv_1f)
+    produce(far_half, spread, send_f)
+    start(0, send_f, recv_1f, 0)
+    start(0, send_f, recv_1f, 2)
+    produce(near_half, spread, send_f)
+    start(0, send_f, recv_1f, 1)
+
+    @pl.loop(3, n - 1)
+    def _(i):
+        start(0, send_f, recv_1f, i)
+
+    recv_1f[me] = send_f[me]
 
     load(gate_hbm, gate, 2).wait()
     load(cot_hbm, cot, 3).wait()
@@ -188,7 +201,7 @@
     def _(e):
         x[e] = (cot[e].astype(f32) * gate[e].astype(f32)).astype(bf16)
 
-    exchange(1, spread, send_b, recv_1b)
+    produce_all(spread, send_b, recv_1b)
 
     quarter = kst.shape[0] // own
 
@@ -210,6 +223,8 @@
                     k * LANES : (k + 1) * LANES,
                 ] = turn[k, pl.ds(e, quarter, stride=own), :].astype(bf16)
 
+    issue(1, send_b, recv_1b, (0, send_f, recv_1f))
+
     load(b_hbm, b, 4).wait()
     wait_arrived(0, send_f, recv_1f)
 
@@ -221,8 +236,8 @@
         second[e] = value
         recv_1f[:, e] = (value * x[e].astype(f32)).astype(bf16).reshape(n, own, width)
 
-    wait_sent(0, send_f, recv_1f)
-    exchange(2, unmix(recv_1f), send_f, recv_2f)
+    produce_all(unmix(recv_1f), send_f, recv_2f)
+    issue(2, send_f, recv_2f, (1, send_b, recv_1b))
 
     wait_arrived(1, send_b, recv_1b)
 
@@ -243,8 +258,7 @@
         device_id_type=MESH,
     )
     swap.start()
-    wait_sent(1, send_b, recv_1b)
-    exchange(3, unmix(recv_1b), send_b, recv_2b)
+    produce_all(unmix(recv_1b), send_b, recv_2b)
 
     swap.wait_recv()
     for side in range(2):
@@ -283,6 +297,8 @@
         for out in outs:
             out.wait()
 
+    issue(3, send_b, recv_2b, (2, send_f, recv_2f))
+
     wait_arrived(2, send_f, recv_2f)
 
     @pl.loop(0, own)
@@ -299,7 +315,6 @@
     out_ggate.start()
 
     swap.wait_send()
-    wait_sent(2, send_f, recv_2f)
     wait_arrived(3, send_b, recv_2b)
 
     def out_row(e):

time: 412 us -> 413 us (level)
  Pallas kernels: 391 us -> 396 us
    pallas_call x1, Pallas kernels: 391 us -> 396 us  [fused_shards(): pl.pallas_call(functools.partial(fused, n), out_shape=(here, here, here,...]
where the time goes in v2:
time: 413 us
  Pallas kernels  396 us (96%)
  local copies, waits for them, and re-layouts  16 us (4%)
    pallas_call x1, Pallas kernels, fused_shards(): pl.pallas_call(functools.partial(fused, n), out_shape=(here, here, here,...  396 us
    unnamed x12, local copies, waits for them, and re-layouts  16 us

profile of v2, /device:TPU:14, one launch (start us, length us, event | category | flops | bytes accessed | tf_op | source)
XLA Modules:
  0.0 412.7 jit_solution(10018457961789541644)
XLA Ops:
  0.6 396.1 %shard_map.93 = (bf16[16,256,512]{2,1,0:T(8,128)(2,1)}, bf16[16,256,512]{2,1,0:T(8,128)(2,1)}, bf16[16,256,512]{2,1,0:T(8,128)(2,1)}, f32[4096,512]{1,0:T(8,128)}, f32[16,256,512]{2,1,0:T(8,128)}) custom-call(bf16[16,256,512]{2,1,0:T(8,128)(2,1)} %bitcast.14, bf16[16,256,512]{2,1,0:T(8,128)(2,1)} %bitcast.15, bf16[4096,512]{1,0:T(8,128)(2,1)} %bitcast.16, ...), custom_call_target="tpu_custom_call" | custom-call | flops 8589934592 | bytes 100663296 | tf_op jit(solution)/shard_map/pallas_call | solution.py:348
  396.7 0.0 copy-start.1
  396.7 4.7 %copy.14 = bf16[1,16,256,512]{3,2,1,0:T(8,128)(2,1)} copy(bf16[1,16,256,512]{3,2,1,0:T(8,128)(2,1)} %bitcast.13) | data formatting | bytes 8388608
  401.4 0.0 copy-done.1
  401.4 0.0 copy-start
  401.4 0.0 slice-start
  401.4 2.1 copy.15
  403.6 1.6 copy-done
  405.1 0.0 slice-start.1
  405.1 2.1 copy.16
  407.3 0.0 slice-done
  407.3 2.1 slice-done.1
  409.3 3.4 copy.17
  (1 shorter events, 0.0 us)
Async XLA Ops:
  396.7 4.7 %copy-start.1 = (bf16[16,256,512]{2,1,0:T(8,128)(2,1)S(1)}, bf16[16,256,512]{2,1,0:T(8,128)(2,1)}, u32[]{:S(2)}) copy-start(bf16[16,256,512]{2,1,0:T(8,128)(2,1)} %get-tuple-element.9) | copy-start | bytes 12582916
  401.4 3.7 copy-start
  401.4 5.8 %slice-start = ((s8[8388608]{0:T(1024)(128)(4,1)}), s8[4194304]{0:T(1024)(128)(4,1)S(1)}, s32[]{:S(2)}) async-start(s8[8388608]{0:T(1024)(128)(4,1)} %bitcast.8), calls=%async_computation | async-start | bytes 8388608
  405.1 4.2 %slice-start.1 = ((s8[8388608]{0:T(1024)(128)(4,1)}), s8[4194304]{0:T(1024)(128)(4,1)S(1)}, s32[]{:S(2)}) async-start(s8[8388608]{0:T(1024)(128)(4,1)} %bitcast.8), calls=%async_computation.1 | async-start | bytes 8388608

commit v3 on v2

--- a/solution.py
+++ b/solution.py
@@ -10,6 +10,7 @@
 MESH = pl.DeviceIdType.MESH
 LANES = 128
 LAG = 2
+PIECES = 4
 
 
 def fused(
@@ -21,7 +22,7 @@
     b_hbm,
     cot_hbm,
     mixed_hbm,
-    gin_hbm,
+    recv_2b,
     ggate_hbm,
     gk_hbm,
     part_hbm,
@@ -35,7 +36,6 @@
     recv_1f,
     recv_1b,
     recv_2f,
-    recv_2b,
     second,
     turn,
     kst,
@@ -43,7 +43,6 @@
     load_sem,
     tmp_sem,
     out_sem,
-    row_sem,
     send_sem,
     recv_sem,
     dp_send,
@@ -139,10 +138,9 @@
         to = order(i)
         message(stage, send, recv, to, to).wait_send()
 
-    def produce_all(product, send, recv):
+    def produce_all(product, send):
         produce(far_half, product, send)
         produce(near_half, product, send)
-        recv[me] = send[me]
 
     def issue(stage, send, recv, before):
         @pl.loop(0, n - 1)
@@ -201,7 +199,8 @@
     def _(e):
         x[e] = (cot[e].astype(f32) * gate[e].astype(f32)).astype(bf16)
 
-    produce_all(spread, send_b, recv_1b)
+    produce_all(spread, send_b)
+    recv_1b[me] = send_b[me]
 
     quarter = kst.shape[0] // own
 
@@ -236,8 +235,10 @@
         second[e] = value
         recv_1f[:, e] = (value * x[e].astype(f32)).astype(bf16).reshape(n, own, width)
 
-    produce_all(unmix(recv_1f), send_f, recv_2f)
+    produce_all(unmix(recv_1f), send_f)
     issue(2, send_f, recv_2f, (1, send_b, recv_1b))
+
+    recv_2f[me] = send_f[me]
 
     wait_arrived(1, send_b, recv_1b)
 
@@ -258,7 +259,9 @@
         device_id_type=MESH,
     )
     swap.start()
-    produce_all(unmix(recv_1b), send_b, recv_2b)
+    produce_all(unmix(recv_1b), send_b)
+    keep = load(send_b.at[me], recv_2b.at[me], 0)
+    keep.start()
 
     swap.wait_recv()
     for side in range(2):
@@ -317,21 +320,76 @@
     swap.wait_send()
     wait_arrived(3, send_b, recv_2b)
 
-    def out_row(e):
-        return pltpu.make_async_copy(x.at[e], gin_hbm.at[e], row_sem.at[e])
-
-    @pl.loop(0, own)
-    def _(e):
-        x[e] = finish(recv_2b, e).astype(bf16)
-        out_row(e).start()
-
     wait_sent(3, send_b, recv_2b)
+    keep.wait()
     out_mixed.wait()
     out_ggate.wait()
 
-    @pl.loop(0, own)
-    def _(e):
-        out_row(e).wait()
+
+def last_rows(
+    a_hbm,
+    held_hbm,
+    mixed_in,
+    ggate_in,
+    gk_in,
+    gin_hbm,
+    mixed_out,
+    ggate_out,
+    gk_out,
+    a,
+    held,
+    rows,
+    in_sem,
+    row_sem,
+    out_sem,
+):
+    sources, targets = (mixed_in, ggate_in, gk_in), (mixed_out, ggate_out, gk_out)
+    pairs = len(sources)
+    own, cols, width = gin_hbm.shape
+
+    def take(e):
+        return pltpu.make_async_copy(held_hbm.at[:, e], held.at[e], in_sem.at[e])
+
+    def give(e):
+        return pltpu.make_async_copy(rows.at[e], gin_hbm.at[e], row_sem.at[e])
+
+    factor = pltpu.make_async_copy(a_hbm, a, in_sem.at[own])
+    factor.start()
+
+    @pl.loop(0, own)
+    def _(e):
+        take(e).start()
+
+    moves = []
+    for i in range(pairs):
+        size = sources[i].shape[0] // PIECES
+        for p in range(PIECES):
+            part = pl.ds(p * size, size)
+            moves.append(
+                pltpu.make_async_copy(
+                    sources[i].at[part], targets[i].at[part], out_sem.at[i, p]
+                )
+            )
+            moves[-1].start()
+    factor.wait()
+
+    @pl.loop(0, own)
+    def _(e):
+        take(e).wait()
+        rows[e] = lax.dot_general(
+            a[e],
+            held[e].reshape(cols, width),
+            (((0,), (0,)), ((), ())),
+            preferred_element_type=jnp.float32,
+        ).astype(rows.dtype)
+        give(e).start()
+
+    @pl.loop(0, own)
+    def _(e):
+        give(e).wait()
+
+    for move in moves:
+        move.wait()
 
 
 def fused_shards(n, inputs, gate, kernel, first_blocks, second_blocks, cotangent):
@@ -345,11 +403,11 @@
     wire = pltpu.VMEM((n, own, own, width), bf16)
     held = pltpu.VMEM((own, cols, width), bf16)
     dma = pltpu.SemaphoreType.DMA
-    mixed, gin, ggate, gk, _ = pl.pallas_call(
+    mixed, blocks, ggate, gk, _ = pl.pallas_call(
         functools.partial(fused, n),
         out_shape=(
             here,
-            here,
+            jax.ShapeDtypeStruct((n, own, own, width), bf16),
             here,
             jax.ShapeDtypeStruct((rows * own, width), f32),
             jax.ShapeDtypeStruct((own, rows, width), f32),
@@ -367,7 +425,6 @@
             wire,
             wire,
             wire,
-            wire,
             pltpu.VMEM((own, rows, width), f32),
             pltpu.VMEM((slabs, cols // 2 * own, LANES), f32),
             pltpu.VMEM((rows // 4 * own, width), bf16),
@@ -375,7 +432,6 @@
             dma((5,)),
             dma((2,)),
             dma((slabs,)),
-            dma((own,)),
             dma((4, n)),
             dma((4, n)),
             dma,
@@ -397,6 +453,27 @@
         second_blocks,
         cotangent.reshape(own, cols, width),
     )
+    grads = jax.ShapeDtypeStruct((rows * own, width), f32)
+    gin, mixed, ggate, gk = pl.pallas_call(
+        last_rows,
+        out_shape=(here, here, here, grads),
+        in_specs=[anywhere] * 5,
+        out_specs=[anywhere] * 4,
+        scratch_shapes=[
+            pltpu.VMEM((own, cols, cols), bf16),
+            pltpu.VMEM((own, n, own, width), bf16),
+            held,
+            dma((own + 1,)),
+            dma((own,)),
+            dma((3, PIECES)),
+        ],
+        compiler_params=pltpu.CompilerParams(vmem_limit_bytes=60 << 20),
+        cost_estimate=pl.CostEstimate(
+            flops=2 * own * cols * cols * width,
+            bytes_accessed=20 * own * cols * width,
+            transcendentals=0,
+        ),
+    )(first_blocks, blocks, mixed, ggate, gk)
     shape = inputs.shape
     return (
         mixed.reshape(shape),

time: 413 us -> 903 us (2.19)
  Pallas kernels: 396 us -> 901 us
  local copies, waits for them, and re-layouts: 16 us -> 0 us
    pallas_call x1 -> x2, Pallas kernels: 396 us -> 901 us  [the longest x1 510 us: fused_shards(): pl.pallas_call(last_rows, out_shape=(here, here, here, grads), in_specs=[...]
    unnamed x12 -> x0, local copies, waits for them, and re-layouts: 16 us -> none
where the time goes in v3:
time: 903 us; the launch traced here: 902 us
  Pallas kernels  901 us (100%)
    pallas_call x1, Pallas kernels, fused_shards(): pl.pallas_call(last_rows, out_shape=(here, here, here, grads), in_specs=[...  510 us
    pallas_call x1, Pallas kernels, fused_shards(): pl.pallas_call(functools.partial(fused, n), out_shape=(here, jax.ShapeDty...  391 us

profile of v3, /device:TPU:14, one launch (start us, length us, event | category | flops | bytes accessed | tf_op | source)
XLA Modules:
  0.0 901.9 jit_solution(7996608761021096604)
XLA Ops:
  0.6 391.4 %shard_map.93 = (bf16[16,256,512]{2,1,0:T(8,128)(2,1)}, bf16[16,16,16,512]{3,2,1,0:T(8,128)(2,1)}, bf16[16,256,512]{2,1,0:T(8,128)(2,1)}, f32[4096,512]{1,0:T(8,128)}, f32[16,256,512]{2,1,0:T(8,128)}) custom-call(bf16[16,256,512]{2,1,0:T(8,128)(2,1)} %bitcast.9, bf16[16,256,512]{2,1,0:T(8,128)(2,1)} %bitcast.10, bf16[4096,512]{1,0:T(8,128)(2,1)} %bitcast.11, ...), custom_call_target="tpu_custom_call" | custom-call | flops 8589934592 | bytes 100663296 | tf_op jit(solution)/shard_map/pallas_call | solution.py:406
  392.1 509.9 %shard_map.94 = (bf16[16,256,512]{2,1,0:T(8,128)(2,1)}, bf16[16,256,512]{2,1,0:T(8,128)(2,1)}, bf16[16,256,512]{2,1,0:T(8,128)(2,1)}, f32[4096,512]{1,0:T(8,128)}) custom-call(bf16[16,256,256]{2,1,0:T(8,128)(2,1)} %a_hbm.3, bf16[16,16,16,512]{3,2,1,0:T(8,128)(2,1)} %get-tuple-element.12.held_hbm, bf16[16,256,512]{2,1,0:T(8,128)(2,1)} %get-tuple-element.13.mixed_in, ...), custom_call_target="tpu_custom_call" | custom-call | flops 1073741824 | bytes 41943040 | tf_op jit(solution)/shard_map/pallas_call | solution.py:457

commit v4 on v3

--- a/solution.py
+++ b/solution.py
@@ -9,7 +9,6 @@
 
 MESH = pl.DeviceIdType.MESH
 LANES = 128
-LAG = 2
 PIECES = 4
 
 
@@ -134,26 +133,16 @@
     def start(stage, send, recv, i):
         message(stage, send, recv, order(i), me).start()
 
-    def left(stage, send, recv, i):
-        to = order(i)
-        message(stage, send, recv, to, to).wait_send()
-
-    def produce_all(product, send):
+    def exchange(stage, product, send, recv):
         produce(far_half, product, send)
+        start(stage, send, recv, 0)
+        start(stage, send, recv, 2)
         produce(near_half, product, send)
-
-    def issue(stage, send, recv, before):
-        @pl.loop(0, n - 1)
+        start(stage, send, recv, 1)
+
+        @pl.loop(3, n - 1)
         def _(i):
-            @pl.when(i >= LAG)
-            def _():
-                left(*before, i - LAG)
-
             start(stage, send, recv, i)
-
-        @pl.loop(n - 1 - LAG, n - 1)
-        def _(i):
-            left(*before, i)
 
     def spread(e, at):
         return jnp.dot(a[e, pl.ds(at, cut), :], x[e], preferred_element_type=f32)
@@ -180,16 +169,7 @@
 
     load(a_hbm, a, 0).wait()
     load(x_hbm, x, 1).wait()
-    produce(far_half, spread, send_f)
-    start(0, send_f, recv_1f, 0)
-    start(0, send_f, recv_1f, 2)
-    produce(near_half, spread, send_f)
-    start(0, send_f, recv_1f, 1)
-
-    @pl.loop(3, n - 1)
-    def _(i):
-        start(0, send_f, recv_1f, i)
-
+    exchange(0, spread, send_f, recv_1f)
     recv_1f[me] = send_f[me]
 
     load(gate_hbm, gate, 2).wait()
@@ -199,7 +179,7 @@
     def _(e):
         x[e] = (cot[e].astype(f32) * gate[e].astype(f32)).astype(bf16)
 
-    produce_all(spread, send_b)
+    exchange(1, spread, send_b, recv_1b)
     recv_1b[me] = send_b[me]
 
     quarter = kst.shape[0] // own
@@ -222,8 +202,6 @@
                     k * LANES : (k + 1) * LANES,
                 ] = turn[k, pl.ds(e, quarter, stride=own), :].astype(bf16)
 
-    issue(1, send_b, recv_1b, (0, send_f, recv_1f))
-
     load(b_hbm, b, 4).wait()
     wait_arrived(0, send_f, recv_1f)
 
@@ -235,8 +213,8 @@
         second[e] = value
         recv_1f[:, e] = (value * x[e].astype(f32)).astype(bf16).reshape(n, own, width)
 
-    produce_all(unmix(recv_1f), send_f)
-    issue(2, send_f, recv_2f, (1, send_b, recv_1b))
+    wait_sent(0, send_f, recv_1f)
+    exchange(2, unmix(recv_1f), send_f, recv_2f)
 
     recv_2f[me] = send_f[me]
 
@@ -259,7 +237,8 @@
         device_id_type=MESH,
     )
     swap.start()
-    produce_all(unmix(recv_1b), send_b)
+    wait_sent(1, send_b, recv_1b)
+    exchange(3, unmix(recv_1b), send_b, recv_2b)
     keep = load(send_b.at[me], recv_2b.at[me], 0)
     keep.start()
 
@@ -300,8 +279,6 @@
         for out in outs:
             out.wait()
 
-    issue(3, send_b, recv_2b, (2, send_f, recv_2f))
-
     wait_arrived(2, send_f, recv_2f)
 
     @pl.loop(0, own)
@@ -320,6 +297,7 @@
     swap.wait_send()
     wait_arrived(3, send_b, recv_2b)
 
+    wait_sent(2, send_f, recv_2f)
     wait_sent(3, send_b, recv_2b)
     keep.wait()
     out_mixed.wait()
@@ -339,12 +317,14 @@
     a,
     held,
     rows,
+    mixed,
+    ggate,
+    gk,
     in_sem,
     row_sem,
+    pass_sem,
     out_sem,
 ):
-    sources, targets = (mixed_in, ggate_in, gk_in), (mixed_out, ggate_out, gk_out)
-    pairs = len(sources)
     own, cols, width = gin_hbm.shape
 
     def take(e):
@@ -353,43 +333,53 @@
     def give(e):
         return pltpu.make_async_copy(rows.at[e], gin_hbm.at[e], row_sem.at[e])
 
-    factor = pltpu.make_async_copy(a_hbm, a, in_sem.at[own])
-    factor.start()
-
-    @pl.loop(0, own)
-    def _(e):
-        take(e).start()
-
-    moves = []
-    for i in range(pairs):
-        size = sources[i].shape[0] // PIECES
+    def through(i, source, stage, target):
+        size = source.shape[0] // PIECES
+        moves = []
         for p in range(PIECES):
             part = pl.ds(p * size, size)
             moves.append(
-                pltpu.make_async_copy(
-                    sources[i].at[part], targets[i].at[part], out_sem.at[i, p]
+                (
+                    pltpu.make_async_copy(
+                        source.at[part], stage.at[part], pass_sem.at[i, p]
+                    ),
+                    pltpu.make_async_copy(
+                        stage.at[part], target.at[part], out_sem.at[i, p]
+                    ),
                 )
             )
-            moves[-1].start()
+        return moves
+
+    moves = (
+        through(0, mixed_in, mixed, mixed_out)
+        + through(1, ggate_in, ggate, ggate_out)
+        + through(2, gk_in, gk, gk_out)
+    )
+    factor = pltpu.make_async_copy(a_hbm, a, in_sem.at[own])
+    factor.start()
+    for e in range(max(own, len(moves))):
+        if e < len(moves):
+            moves[e][0].start()
+        if e < own:
+            take(e).start()
     factor.wait()
-
-    @pl.loop(0, own)
-    def _(e):
-        take(e).wait()
-        rows[e] = lax.dot_general(
-            a[e],
-            held[e].reshape(cols, width),
-            (((0,), (0,)), ((), ())),
-            preferred_element_type=jnp.float32,
-        ).astype(rows.dtype)
-        give(e).start()
-
-    @pl.loop(0, own)
-    def _(e):
+    for e in range(max(own, len(moves))):
+        if e < len(moves):
+            moves[e][0].wait()
+            moves[e][1].start()
+        if e < own:
+            take(e).wait()
+            rows[e] = lax.dot_general(
+                a[e],
+                held[e].reshape(cols, width),
+                (((0,), (0,)), ((), ())),
+                preferred_element_type=jnp.float32,
+            ).astype(rows.dtype)
+            give(e).start()
+    for e in range(own):
         give(e).wait()
-
     for move in moves:
-        move.wait()
+        move[1].wait()
 
 
 def fused_shards(n, inputs, gate, kernel, first_blocks, second_blocks, cotangent):
@@ -463,8 +453,12 @@
             pltpu.VMEM((own, cols, cols), bf16),
             pltpu.VMEM((own, n, own, width), bf16),
             held,
+            held,
+            held,
+            pltpu.VMEM((rows * own, width), f32),
             dma((own + 1,)),
             dma((own,)),
+            dma((3, PIECES)),
             dma((3, PIECES)),
         ],
         compiler_params=pltpu.CompilerParams(vmem_limit_bytes=60 << 20),

time: 903 us -> 407 us (0.45)
  Pallas kernels: 901 us -> 405 us
    pallas_call x1, Pallas kernels: 510 us -> 16.3 us  [fused_shards(): pl.pallas_call(last_rows, out_shape=(here, here, here, grads), in_specs=[...]
where the time goes in v4:
time: 407 us; the launch traced here: 406 us
  Pallas kernels  405 us (100%)
    pallas_call x1, Pallas kernels, fused_shards(): pl.pallas_call(functools.partial(fused, n), out_shape=(here, jax.ShapeDty...  389 us
    pallas_call x1, Pallas kernels, fused_shards(): pl.pallas_call(last_rows, out_shape=(here, here, here, grads), in_specs=[...  16.3 us

profile of v4, /device:TPU:14, one launch (start us, length us, event | category | flops | bytes accessed | tf_op | source)
XLA Modules:
  0.0 406.0 jit_solution(3403201944488511170)
XLA Ops:
  0.6 389.1 %shard_map.93 = (bf16[16,256,512]{2,1,0:T(8,128)(2,1)}, bf16[16,16,16,512]{3,2,1,0:T(8,128)(2,1)}, bf16[16,256,512]{2,1,0:T(8,128)(2,1)}, f32[4096,512]{1,0:T(8,128)}, f32[16,256,512]{2,1,0:T(8,128)}) custom-call(bf16[16,256,512]{2,1,0:T(8,128)(2,1)} %bitcast.9, bf16[16,256,512]{2,1,0:T(8,128)(2,1)} %bitcast.10, bf16[4096,512]{1,0:T(8,128)(2,1)} %bitcast.11, ...), custom_call_target="tpu_custom_call" | custom-call | flops 8589934592 | bytes 100663296 | tf_op jit(solution)/shard_map/pallas_call | solution.py:396
  389.7 16.3 %shard_map.94 = (bf16[16,256,512]{2,1,0:T(8,128)(2,1)}, bf16[16,256,512]{2,1,0:T(8,128)(2,1)}, bf16[16,256,512]{2,1,0:T(8,128)(2,1)}, f32[4096,512]{1,0:T(8,128)}) custom-call(bf16[16,256,256]{2,1,0:T(8,128)(2,1)} %a_hbm.3, bf16[16,16,16,512]{3,2,1,0:T(8,128)(2,1)} %get-tuple-element.12.held_hbm, bf16[16,256,512]{2,1,0:T(8,128)(2,1)} %get-tuple-element.13.mixed_in, ...), custom_call_target="tpu_custom_call" | custom-call | flops 1073741824 | bytes 41943040 | tf_op jit(solution)/shard_map/pallas_call | solution.py:447

commit v5 on v4

--- a/solution.py
+++ b/solution.py
@@ -66,9 +66,6 @@
 
     load(a_hbm, a, 0).start()
     load(x_hbm, x, 1).start()
-    load(gate_hbm, gate, 2).start()
-    load(cot_hbm, cot, 3).start()
-    load(b_hbm, b, 4).start()
 
     barrier = pltpu.get_barrier_semaphore()
 
@@ -169,6 +166,9 @@
 
     load(a_hbm, a, 0).wait()
     load(x_hbm, x, 1).wait()
+    load(gate_hbm, gate, 2).start()
+    load(cot_hbm, cot, 3).start()
+    load(b_hbm, b, 4).start()
     exchange(0, spread, send_f, recv_1f)
     recv_1f[me] = send_f[me]
 

time: 407 us -> 406 us (level)
  no operation moved by 1% of the time
where the time goes in v5:
time: 406 us
  Pallas kernels  405 us (100%)
    pallas_call x1, Pallas kernels, fused_shards(): pl.pallas_call(functools.partial(fused, n), out_shape=(here, jax.ShapeDty...  389 us
    pallas_call x1, Pallas kernels, fused_shards(): pl.pallas_call(last_rows, out_shape=(here, here, here, grads), in_specs=[...  16.3 us

profile of v5, /device:TPU:14, one launch (start us, length us, event | category | flops | bytes accessed | tf_op | source)
XLA Modules:
  0.0 405.6 jit_solution(1897976084931138049)
XLA Ops:
  0.6 388.7 %shard_map.93 = (bf16[16,256,512]{2,1,0:T(8,128)(2,1)}, bf16[16,16,16,512]{3,2,1,0:T(8,128)(2,1)}, bf16[16,256,512]{2,1,0:T(8,128)(2,1)}, f32[4096,512]{1,0:T(8,128)}, f32[16,256,512]{2,1,0:T(8,128)}) custom-call(bf16[16,256,512]{2,1,0:T(8,128)(2,1)} %bitcast.9, bf16[16,256,512]{2,1,0:T(8,128)(2,1)} %bitcast.10, bf16[4096,512]{1,0:T(8,128)(2,1)} %bitcast.11, ...), custom_call_target="tpu_custom_call" | custom-call | flops 8589934592 | bytes 100663296 | tf_op jit(solution)/shard_map/pallas_call | solution.py:396
  389.3 16.3 %shard_map.94 = (bf16[16,256,512]{2,1,0:T(8,128)(2,1)}, bf16[16,256,512]{2,1,0:T(8,128)(2,1)}, bf16[16,256,512]{2,1,0:T(8,128)(2,1)}, f32[4096,512]{1,0:T(8,128)}) custom-call(bf16[16,256,256]{2,1,0:T(8,128)(2,1)} %a_hbm.3, bf16[16,16,16,512]{3,2,1,0:T(8,128)(2,1)} %get-tuple-element.12.held_hbm, bf16[16,256,512]{2,1,0:T(8,128)(2,1)} %get-tuple-element.13.mixed_in, ...), custom_call_target="tpu_custom_call" | custom-call | flops 1073741824 | bytes 41943040 | tf_op jit(solution)/shard_map/pallas_call | solution.py:447
